TPU v7x, 256 devices: a whole 4x4x8 slice. The times are simulated.
256 devices in a mesh: row: 16 (over z_lo, x), col: 16 (over z_hi, y, core).
Axes of the slice: x: 4, y: 4, z: 8 (z_hi: 2, z_lo: 4; z = z_hi * 4 + z_lo), core: 2. Of those that a mesh axis runs over, the one named last changes fastest.
Arguments:
- inverse_tiles: bfloat16 [16384, 16384], P('row', 'col'), may hold values from -0.046875 to 0.046875
- factor: bfloat16 [16384, 4, 512], P('row', None, 'col'), may hold values from -0.75 to 0.75
- inverse_diag: float32 [4, 512, 512], P(None, 'row', 'col'), may hold values from -6 to 6
- tile_list: int32 [4, 128], replicated, may hold values from 0 to 127, as said below
- tile_count: int32 [4], replicated, may hold values from 86 to 128, as said below
Outputs:
- inverse_panel: bfloat16 [16384, 4, 512], P(('row', 'col'))
- diag_block: float32 [4, 512, 512], P(None, 'row', 'col')
Inputs may be any that keep to these rules, and one draw needn't show every extreme that they name: For each supernode the first tile_count entries of tile_list name distinct tiles in increasing order; the remaining entries name the tiles that are not listed. `tile_count`: some supernode lists all 128 tiles.
All inputs are finite; a program needn't handle non-finite values.
Results may differ from a plain program's by a relative error of at most 0.014.
Values may be sent and summed in bfloat16 or wider, within the bound.
A program may use at most 64 MiB of HBM per device.

v0:
```python
import jax
import jax.numpy as jnp
from jax import lax
from jax.sharding import Mesh
from jax.sharding import PartitionSpec as P

TILE = 128
COL = ("col_0", "col_1", "col_2")
ROW_COL = ("row", "col_0", "col_1", "col_2")


def spread(x, axis, root):
    mine = lax.axis_index(axis) == root
    return lax.psum(jnp.where(mine, x, jnp.zeros_like(x)), axis)


def split_up(x, dim, size):
    before, after = (x.shape[:dim], x.shape[dim + 1 :])
    return jnp.moveaxis(x.reshape(*before, size, -1, *after), dim, 0)


def summed_rows(x, chips, core, dim):
    sizes = (lax.axis_size(chips), lax.axis_size(core))
    blocks = split_up(x, dim, sizes[0] * sizes[1])
    inside = blocks.shape[1:]
    blocks = blocks.reshape(*sizes, *inside).swapaxes(0, 1).reshape(-1, *inside)
    blocks = lax.psum_scatter(blocks, core, scatter_dimension=0, tiled=True)
    return lax.psum_scatter(blocks, chips, scatter_dimension=0, tiled=True)[0]


def sent_and_summed(x, axis, dim):
    blocks = split_up(x, dim, lax.axis_size(axis))
    arrived = lax.all_to_all(blocks, axis, split_axis=0, concat_axis=0, tiled=True)
    return arrived.astype(jnp.float32).sum(axis=0)


def per_device(inverse_tiles, factor, inverse_diag, tile_list, tile_count):
    row_devices = lax.axis_size("row")
    col_devices = lax.axis_size(COL)
    row_index = lax.axis_index("row")
    col_index = lax.axis_index(COL)
    rows_blk = inverse_tiles.shape[0]
    cols_blk = inverse_tiles.shape[1]
    supers = factor.shape[1]
    panel_width = factor.shape[2] * col_devices
    tile_total = tile_list.shape[1]
    position = jnp.arange(tile_total, dtype=jnp.int32)
    matches = (tile_list[:, :, None] == position[None, None, :]) & (
        position[None, :, None] < tile_count[:, None, None]
    )
    listed = jnp.any(matches, axis=1).astype(jnp.float32)
    live_all = jnp.repeat(listed, TILE, axis=1)
    row_live = lax.dynamic_slice_in_dim(live_all, row_index * rows_blk, rows_blk, 1).T
    row_factor = lax.all_gather(factor, COL, axis=2, tiled=True)
    row_factor = jnp.where(row_live[:, :, None] > 0, row_factor, jnp.zeros_like(row_factor))
    blocks_per = row_devices // col_devices
    received = spread(row_factor, "row", col_index * blocks_per + 0)
    col_factor = received.reshape(cols_blk, supers * panel_width)
    whole_term = jnp.dot(inverse_tiles, col_factor, preferred_element_type=jnp.float32).reshape(
        rows_blk, supers, panel_width
    )
    panel_cols = summed_rows(whole_term, ("col_0", "col_1"), "col_2", 2)
    panel_cols = -panel_cols * row_live[:, :, None]
    diag_part = jnp.einsum(
        "rsv,rsw->svw", row_factor.astype(jnp.float32), panel_cols, precision=lax.Precision.HIGHEST
    )
    diag_mine = sent_and_summed(diag_part.astype(jnp.bfloat16), "row", 1)
    inverse_panel = lax.all_to_all(
        panel_cols.astype(jnp.bfloat16), COL, split_axis=0, concat_axis=2, tiled=True
    )
    diag_block = inverse_diag - diag_mine
    return (inverse_panel, diag_block)


def solution(mesh):
    torus = Mesh(
        mesh.devices.reshape(mesh.shape["row"], 2, 4, 2), ("row", "col_0", "col_1", "col_2")
    )
    return jax.shard_map(
        per_device,
        mesh=torus,
        in_specs=(P("row", COL), P("row", None, COL), P(None, "row", COL), P(), P()),
        out_specs=(P(ROW_COL, None, None), P(None, "row", COL)),
        check_vma=False,
    )
```

profile of v0, /device:TPU:32, one launch (start us, length us, event | category | flops | bytes accessed | tf_op | source)
XLA Modules:
  0.0 482.2 jit_solution(6248333700501249892)
XLA Ops:
  7.2 0.0 copy-start
  7.2 0.0 all-gather.2.cloned.1.call-start
  7.2 0.7 all-gather.2.cloned.1.call-update
  7.9 0.0 all-reduce.2.cloned.1.call-start
  8.0 0.7 iota_compare_fusion.1
  8.7 0.9 fusion.6
  9.6 0.1 broadcast_bitcast_fusion
  9.7 0.2 copy.57
  9.9 79.6 %all-gather.2.cloned.1.call-done = bf16[1024,4,512]{0,2,1:T(8,128)(2,1)} async-done(((bf16[1024,4,32]{0,2,1:T(8,128)(2,1)}), bf16[1024,4,512]{0,2,1:T(8,128)(2,1)}) %all-gather.2.cloned.1.call-update) | async-done | bytes 4194320 | tf_op jit(solution)/shard_map/all_gather | solution.py:54
  89.5 4.5 broadcast_select_fusion.1
  94.1 0.0 all-reduce.2.cloned.1.call-update
  94.1 0.0 reduce-scatter.3.cloned.1.call-start
  94.1 169.6 %all-reduce.2.cloned.1.call-done = bf16[1024,2048]{0,1:T(8,128)(2,1)} async-done(((bf16[1024,2048]{0,1:T(8,128)(2,1)}), bf16[1024,2048]{0,1:T(8,128)(2,1)}) %all-reduce.2.cloned.1.call-update) | async-done | bytes 4194320 | tf_op jit(solution)/shard_map/psum | solution.py:14
  263.7 0.0 copy-done
  263.7 6.4 %fusion.9 = f32[2048,1024]{1,0:T(8,128)S(1)} fusion(bf16[1024,2048]{0,1:T(8,128)(2,1)} %all-reduce.2.cloned.1.call-done, bf16[1024,1024]{1,0:T(8,128)(2,1)S(1)} %copy-done), kind=kOutput, calls=%fused_computation.20 | convolution fusion | flops 4294967296 | bytes 14680064 | tf_op jit(solution)/shard_map/dot_general | solution.py:59
  270.1 4.1 copy.38
  274.2 0.0 reduce-scatter.3.cloned.1.call-update
  274.2 0.0 reduce-scatter.5.cloned.1.call-start
  274.3 25.8 %reduce-scatter.3.cloned.1.call-done = f32[8,1024,4,32]{1,3,2,0:T(8,128)} async-done(((f32[16,1024,4,32]{1,3,2,0:T(8,128)}), f32[8,1024,4,32]{1,3,2,0:T(8,128)}) %reduce-scatter.3.cloned.1.call-update) | async-done | bytes 4194320 | tf_op jit(solution)/shard_map/reduce_scatter | solution.py:27
  300.1 0.0 reduce-scatter.5.cloned.1.call-update
  300.1 131.2 %reduce-scatter.5.cloned.1.call-done = f32[1,1024,4,32]{1,3,2,0:T(8,128)} async-done(((f32[8,1024,4,32]{1,3,2,0:T(8,128)}), f32[1,1024,4,32]{1,3,2,0:T(8,128)}) %reduce-scatter.5.cloned.1.call-update) | async-done | bytes 524304 | tf_op jit(solution)/shard_map/reduce_scatter | solution.py:28
  431.3 6.0 %fusion.2 = bf16[4,512,32]{1,2,0:T(8,128)(2,1)S(1)} fusion(bf16[1024,4,512]{0,2,1:T(8,128)(2,1)} %all-gather.2.cloned.1.call-done, pred[1024,4]{0,1:T(4,128)(4,1)S(1)} %get-tuple-element.12, f32[1,1024,4,32]{1,3,2,0:T(8,128)} %reduce-scatter.5.cloned.1.call-done, f32[1024,4]{0,1:T(4,128)S(1)} %get-tuple-element.13), kind=kOutput, calls=%fused_computation.4 | convolution fusion | flops 807731200 | bytes 4870144 | tf_op jit(solution)/shard_map/rsv,rsw->svw/dot_general | solution.py:64
  437.3 0.3 reshape.53
  437.6 0.1 copy.58
  437.7 1.2 reshape.56
  438.9 5.8 %all-to-all-start.1 = ((bf16[16,2,2048]{2,1,0:T(2,128)(2,1)}), bf16[16,2,2048]{2,1,0:T(2,128)(2,1)S(1)}, u32[]{:S(2)}, u32[]{:S(2)}) async-start(bf16[16,2,2048]{2,1,0:T(2,128)(2,1)} %reshape.56), calls=%async_computation.3 | async-start | bytes 262144 | tf_op jit(solution)/shard_map/all_to_all | solution.py:33
  444.7 1.1 fusion.3
  445.8 0.7 copy.39
  446.5 1.7 reshape.54
  448.2 3.4 all-to-all-done.1
  451.6 5.4 %all-to-all-start = ((bf16[16,2,4096]{2,1,0:T(2,128)(2,1)}), bf16[16,2,4096]{2,1,0:T(2,128)(2,1)S(1)}, u32[]{:S(2)}, u32[]{:S(2)}) async-start(bf16[16,2,4096]{2,1,0:T(2,128)(2,1)} %reshape.54), calls=%async_computation.2 | async-start | bytes 524288 | tf_op jit(solution)/shard_map/all_to_all | solution.py:68
  457.0 0.9 copy.45
  457.9 0.3 reshape.57
  458.2 0.1 convert_reduce_fusion
  458.3 0.7 copy.47
  459.1 12.7 %all-to-all-done = bf16[16,2,4096]{2,1,0:T(2,128)(2,1)S(1)} async-done(((bf16[16,2,4096]{2,1,0:T(2,128)(2,1)}), bf16[16,2,4096]{2,1,0:T(2,128)(2,1)S(1)}, u32[]{:S(2)}, u32[]{:S(2)}) %all-to-all-start) | async-done | bytes 262176 | tf_op jit(solution)/shard_map/all_to_all | solution.py:68
  471.8 0.5 reshape.55
  472.3 1.3 copy.50
  473.6 2.0 copy.46
  (3 shorter events, 0.0 us)
Async XLA Ops:
  7.2 256.6 %copy-start = (bf16[1024,1024]{1,0:T(8,128)(2,1)S(1)}, bf16[1024,1024]{1,0:T(8,128)(2,1)}, u32[]{:S(2)}) copy-start(bf16[1024,1024]{1,0:T(8,128)(2,1)} %param.5) | copy-start | bytes 6291460
  7.2 82.4 %all-gather.2.cloned.1.call-start = ((), (), s32[]{:S(2)}) async-start(), calls=%async_computation.4 | async-start | bytes 4456448 | tf_op jit(solution)/shard_map/all_gather | solution.py:54
  7.9 255.8 %all-reduce.2.cloned.1.call-start = ((), (), s32[]{:S(2)}) async-start(), calls=%async_computation.5 | async-start | bytes 8388608 | tf_op jit(solution)/shard_map/psum | solution.py:14
  94.1 206.0 %reduce-scatter.3.cloned.1.call-start = ((), (), s32[]{:S(2)}) async-start(), calls=%async_computation.6 | async-start | bytes 12582912 | tf_op jit(solution)/shard_map/reduce_scatter | solution.py:27
  274.2 157.1 %reduce-scatter.5.cloned.1.call-start = ((), (), s32[]{:S(2)}) async-start(), calls=%async_computation.7 | async-start | bytes 4718592 | tf_op jit(solution)/shard_map/reduce_scatter | solution.py:28
  438.9 12.7 %all-to-all-start.1 = ((bf16[16,2,2048]{2,1,0:T(2,128)(2,1)}), bf16[16,2,2048]{2,1,0:T(2,128)(2,1)S(1)}, u32[]{:S(2)}, u32[]{:S(2)}) async-start(bf16[16,2,2048]{2,1,0:T(2,128)(2,1)} %reshape.56), calls=%async_computation.3 | async-start | bytes 262144 | tf_op jit(solution)/shard_map/all_to_all | solution.py:33
  451.6 20.2 %all-to-all-start = ((bf16[16,2,4096]{2,1,0:T(2,128)(2,1)}), bf16[16,2,4096]{2,1,0:T(2,128)(2,1)S(1)}, u32[]{:S(2)}, u32[]{:S(2)}) async-start(bf16[16,2,4096]{2,1,0:T(2,128)(2,1)} %reshape.54), calls=%async_computation.2 | async-start | bytes 524288 | tf_op jit(solution)/shard_map/all_to_all | solution.py:68
Sparse Core Ops, SparseCore 0:
  10.8 78.7 all-gather.1
  94.2 169.4 all-reduce.1
  274.3 25.6 reduce-scatter.2
  304.6 126.5 reduce-scatter.4
where the time goes:
time: 483 us; the launch traced here: 482 us
  waiting for transfers between devices  423 us (88%)
  local copies, waits for them, and re-layouts  14.1 us (3%)
  between operations  13.9 us (3%)
  matrix products  12.3 us (3%)
  starting transfers between devices  11.4 us (2%)
  other arithmetic  7.39 us (2%)
    psum x1, waiting for transfers between devices, spread(): return lax.psum(jnp.where(mine, x, jnp.zeros_like(x)), axis)  170 us
    reduce_scatter x1, waiting for transfers between devices, summed_rows(): return lax.psum_scatter(blocks, chips, scatter_dimension=0, tiled=True)[0]  131 us
    all_gather x1, waiting for transfers between devices, per_device(): row_factor = lax.all_gather(factor, COL, axis=2, tiled=True)  79.6 us
    reduce_scatter x1, waiting for transfers between devices, summed_rows(): blocks = lax.psum_scatter(blocks, core, scatter_dimension=0, tiled=True)  25.8 us
    all_to_all x1, waiting for transfers between devices, per_device(): lax.all_to_all(panel_cols.astype(jnp.bfloat16), COL, split_axis=0, concat...  12.7 us
  transfers between devices with their start and end apart: 6, of which 6 were waited for; matrix products, arithmetic and copies ran while one was open for 2% of the time, Pallas kernels for 0%

commit v1 on v0

--- a/solution.py
+++ b/solution.py
@@ -51,7 +51,9 @@
     listed = jnp.any(matches, axis=1).astype(jnp.float32)
     live_all = jnp.repeat(listed, TILE, axis=1)
     row_live = lax.dynamic_slice_in_dim(live_all, row_index * rows_blk, rows_blk, 1).T
-    row_factor = lax.all_gather(factor, COL, axis=2, tiled=True)
+    row_factor = jnp.concatenate(
+        lax.all_to_all(jnp.stack([factor] * lax.axis_size(COL)), COL, 0, 0), axis=2
+    )
     row_factor = jnp.where(row_live[:, :, None] > 0, row_factor, jnp.zeros_like(row_factor))
     blocks_per = row_devices // col_devices
     received = spread(row_factor, "row", col_index * blocks_per + 0)

time: 483 us -> 526 us (1.089)
  waiting for transfers between devices: 423 us -> 450 us
  starting transfers between devices: 11.4 us -> 21.8 us
  local copies, waits for them, and re-layouts: 14.1 us -> 22.3 us
    all_to_all x0 -> x1, waiting for transfers between devices: none -> 98.4 us  [per_device(): lax.all_to_all(jnp.stack([factor] * lax.axis_size(COL)), COL, 0, 0)]
    all_gather x1 -> x0, waiting for transfers between devices: 79.6 us -> none  [per_device(): row_factor = lax.all_gather(factor, COL, axis=2, tiled=True)]
    all_to_all x0 -> x1, starting transfers between devices: none -> 10.5 us  [per_device(): lax.all_to_all(jnp.stack([factor] * lax.axis_size(COL)), COL, 0, 0)]
    psum x1, waiting for transfers between devices: 170 us -> 177 us  [spread(): return lax.psum(jnp.where(mine, x, jnp.zeros_like(x)), axis)]
  transfers between devices with their start and end apart: 6 -> 6, of which waited for: 6 -> 6; matrix products, arithmetic and copies ran while one was open for 2% -> 1% of each run, Pallas kernels for 0% -> 0%
where the time goes in v1:
time: 526 us; the launch traced here: 525 us
  waiting for transfers between devices  450 us (86%)
  local copies, waits for them, and re-layouts  22.3 us (4%)
  starting transfers between devices  21.8 us (4%)
  between operations  13.9 us (3%)
  matrix products  12.4 us (2%)
    psum x1, waiting for transfers between devices, spread(): return lax.psum(jnp.where(mine, x, jnp.zeros_like(x)), axis)  177 us
    reduce_scatter x1, waiting for transfers between devices, summed_rows(): return lax.psum_scatter(blocks, chips, scatter_dimension=0, tiled=True)[0]  131 us
    all_to_all x1, waiting for transfers between devices, per_device(): lax.all_to_all(jnp.stack([factor] * lax.axis_size(COL)), COL, 0, 0)  98.4 us
    reduce_scatter x1, waiting for transfers between devices, summed_rows(): blocks = lax.psum_scatter(blocks, core, scatter_dimension=0, tiled=True)  25.8 us
    all_to_all x1, waiting for transfers between devices, per_device(): lax.all_to_all(panel_cols.astype(jnp.bfloat16), COL, split_axis=0, concat...  12.7 us
  transfers between devices with their start and end apart: 6, of which 6 were waited for; matrix products, arithmetic and copies ran while one was open for 1% of the time, Pallas kernels for 0%

profile of v1, /device:TPU:32, one launch (start us, length us, event | category | flops | bytes accessed | tf_op | source)
XLA Modules:
  0.0 525.2 jit_solution(12575848480808284486)
XLA Ops:
  7.2 0.0 copy-start
  7.2 3.6 stack.2
  10.8 0.0 copy-start.3
  10.8 0.0 copy-start.2
  10.8 10.5 %all-to-all-start = ((bf16[16,1024,4,32]{1,3,2,0:T(8,128)(2,1)}), bf16[16,1024,4,32]{1,3,2,0:T(8,128)(2,1)}, u32[]{:S(2)}, u32[]{:S(2)}) async-start(bf16[16,1024,4,32]{1,3,2,0:T(8,128)(2,1)} %stack.2), calls=%async_computation | async-start | bytes 8388608 | tf_op jit(solution)/shard_map/all_to_all | solution.py:55
  21.3 0.0 all-reduce.2.cloned.1.call-start
  21.3 0.0 copy-done.3
  21.3 0.1 iota_compare_fusion.1
  21.4 0.0 copy-done.2
  21.4 0.2 fusion.3
  21.7 0.1 broadcast_bitcast_fusion
  21.8 0.2 copy.60
  22.0 98.4 %all-to-all-done = bf16[16,1024,4,32]{1,3,2,0:T(8,128)(2,1)} async-done(((bf16[16,1024,4,32]{1,3,2,0:T(8,128)(2,1)}), bf16[16,1024,4,32]{1,3,2,0:T(8,128)(2,1)}, u32[]{:S(2)}, u32[]{:S(2)}) %all-to-all-start) | async-done | bytes 4194336 | tf_op jit(solution)/shard_map/all_to_all | solution.py:55
  120.4 2.7 copy.40
  123.2 4.0 broadcast_select_fusion
  127.2 0.0 all-reduce.2.cloned.1.call-update
  127.2 0.0 reduce-scatter.3.cloned.1.call-start
  127.3 177.4 %all-reduce.2.cloned.1.call-done = bf16[1024,2048]{0,1:T(8,128)(2,1)} async-done(((bf16[1024,2048]{0,1:T(8,128)(2,1)}), bf16[1024,2048]{0,1:T(8,128)(2,1)}) %all-reduce.2.cloned.1.call-update) | async-done | bytes 4194320 | tf_op jit(solution)/shard_map/psum | solution.py:14
  304.7 0.0 copy-done
  304.7 6.4 %fusion.5 = f32[2048,1024]{1,0:T(8,128)S(1)} fusion(bf16[1024,2048]{0,1:T(8,128)(2,1)} %all-reduce.2.cloned.1.call-done, bf16[1024,1024]{1,0:T(8,128)(2,1)S(1)} %copy-done), kind=kOutput, calls=%fused_computation.17 | convolution fusion | flops 4294967296 | bytes 14680064 | tf_op jit(solution)/shard_map/dot_general | solution.py:61
  311.0 4.1 copy.41
  315.1 0.0 reduce-scatter.3.cloned.1.call-update
  315.1 0.0 reduce-scatter.5.cloned.1.call-start
  315.2 25.8 %reduce-scatter.3.cloned.1.call-done = f32[8,1024,4,32]{1,3,2,0:T(8,128)} async-done(((f32[16,1024,4,32]{1,3,2,0:T(8,128)}), f32[8,1024,4,32]{1,3,2,0:T(8,128)}) %reduce-scatter.3.cloned.1.call-update) | async-done | bytes 4194320 | tf_op jit(solution)/shard_map/reduce_scatter | solution.py:27
  340.9 0.0 reduce-scatter.5.cloned.1.call-update
  341.0 131.5 %reduce-scatter.5.cloned.1.call-done = f32[1,1024,4,32]{1,3,2,0:T(8,128)} async-done(((f32[8,1024,4,32]{1,3,2,0:T(8,128)}), f32[1,1024,4,32]{1,3,2,0:T(8,128)}) %reduce-scatter.5.cloned.1.call-update) | async-done | bytes 524304 | tf_op jit(solution)/shard_map/reduce_scatter | solution.py:28
  472.5 0.0 copy-start.1
  472.5 6.1 %convolution_convert_fusion = bf16[4,512,32]{1,2,0:T(8,128)(2,1)S(1)} fusion(bf16[1024,4,512]{0,2,1:T(8,128)(2,1)} %get-tuple-element.13, f32[1,1024,4,32]{1,3,2,0:T(8,128)} %reduce-scatter.5.cloned.1.call-done, f32[1024,4]{0,1:T(4,128)S(1)} %get-tuple-element.15), kind=kOutput, calls=%fused_computation.2 | convolution fusion | flops 805634048 | bytes 4866048 | tf_op jit(solution)/shard_map/rsv,rsw->svw/dot_general | solution.py:66
  478.5 0.3 reshape.63
  478.8 0.9 copy.61
  479.7 2.2 reshape.66
  482.0 5.8 %all-to-all-start.2 = ((bf16[16,2,2048]{2,1,0:T(2,128)(2,1)}), bf16[16,2,2048]{2,1,0:T(2,128)(2,1)S(1)}, u32[]{:S(2)}, u32[]{:S(2)}) async-start(bf16[16,2,2048]{2,1,0:T(2,128)(2,1)} %reshape.66), calls=%async_computation.4 | async-start | bytes 262144 | tf_op jit(solution)/shard_map/all_to_all | solution.py:33
  487.7 0.0 copy-done.1
  487.7 0.1 fusion
  487.8 0.7 copy.42
  488.5 1.7 reshape.64
  490.2 4.4 all-to-all-done.2
  494.7 5.4 %all-to-all-start.1 = ((bf16[16,2,4096]{2,1,0:T(2,128)(2,1)}), bf16[16,2,4096]{2,1,0:T(2,128)(2,1)S(1)}, u32[]{:S(2)}, u32[]{:S(2)}) async-start(bf16[16,2,4096]{2,1,0:T(2,128)(2,1)} %reshape.64), calls=%async_computation.3 | async-start | bytes 524288 | tf_op jit(solution)/shard_map/all_to_all | solution.py:70
  500.1 0.9 copy.48
  501.0 0.3 reshape.67
  501.3 0.1 convert_reduce_fusion
  501.4 0.7 copy.50
  502.1 12.7 %all-to-all-done.1 = bf16[16,2,4096]{2,1,0:T(2,128)(2,1)S(1)} async-done(((bf16[16,2,4096]{2,1,0:T(2,128)(2,1)}), bf16[16,2,4096]{2,1,0:T(2,128)(2,1)S(1)}, u32[]{:S(2)}, u32[]{:S(2)}) %all-to-all-start.1) | async-done | bytes 262176 | tf_op jit(solution)/shard_map/all_to_all | solution.py:70
  514.8 0.5 reshape.65
  515.3 1.3 copy.53
  516.7 2.0 copy.49
  (3 shorter events, 0.0 us)
Async XLA Ops:
  7.2 297.5 %copy-start = (bf16[1024,1024]{1,0:T(8,128)(2,1)S(1)}, bf16[1024,1024]{1,0:T(8,128)(2,1)}, u32[]{:S(2)}) copy-start(bf16[1024,1024]{1,0:T(8,128)(2,1)} %param.5) | copy-start | bytes 6291460
  10.8 10.6 %copy-start.3 = (s32[4]{0:T(128)S(1)}, s32[4]{0:T(128)}, u32[]{:S(2)}) copy-start(s32[4]{0:T(128)} %param.9) | copy-start | bytes 52
  10.8 10.6 %copy-start.2 = (s32[4,128]{1,0:T(4,128)S(1)}, s32[4,128]{1,0:T(4,128)}, u32[]{:S(2)}) copy-start(s32[4,128]{1,0:T(4,128)} %param.8) | copy-start | bytes 6148
  10.8 109.7 %all-to-all-start = ((bf16[16,1024,4,32]{1,3,2,0:T(8,128)(2,1)}), bf16[16,1024,4,32]{1,3,2,0:T(8,128)(2,1)}, u32[]{:S(2)}, u32[]{:S(2)}) async-start(bf16[16,1024,4,32]{1,3,2,0:T(8,128)(2,1)} %stack.2), calls=%async_computation | async-start | bytes 8388608 | tf_op jit(solution)/shard_map/all_to_all | solution.py:55
  21.3 283.4 %all-reduce.2.cloned.1.call-start = ((), (), s32[]{:S(2)}) async-start(), calls=%async_computation.5 | async-start | bytes 8388608 | tf_op jit(solution)/shard_map/psum | solution.py:14
  127.2 213.7 %reduce-scatter.3.cloned.1.call-start = ((), (), s32[]{:S(2)}) async-start(), calls=%async_computation.6 | async-start | bytes 12582912 | tf_op jit(solution)/shard_map/reduce_scatter | solution.py:27
  315.1 157.3 %reduce-scatter.5.cloned.1.call-start = ((), (), s32[]{:S(2)}) async-start(), calls=%async_computation.7 | async-start | bytes 4718592 | tf_op jit(solution)/shard_map/reduce_scatter | solution.py:28
  472.5 15.3 %copy-start.1 = (f32[1,1024,4,32]{1,3,2,0:T(8,128)S(1)}, f32[1,1024,4,32]{1,3,2,0:T(8,128)}, u32[]{:S(2)}) copy-start(f32[1,1024,4,32]{1,3,2,0:T(8,128)} %reduce-scatter.5.cloned.1.call-done) | copy-start | bytes 1572868
  482.0 12.7 %all-to-all-start.2 = ((bf16[16,2,2048]{2,1,0:T(2,128)(2,1)}), bf16[16,2,2048]{2,1,0:T(2,128)(2,1)S(1)}, u32[]{:S(2)}, u32[]{:S(2)}) async-start(bf16[16,2,2048]{2,1,0:T(2,128)(2,1)} %reshape.66), calls=%async_computation.4 | async-start | bytes 262144 | tf_op jit(solution)/shard_map/all_to_all | solution.py:33
  494.7 20.2 %all-to-all-start.1 = ((bf16[16,2,4096]{2,1,0:T(2,128)(2,1)}), bf16[16,2,4096]{2,1,0:T(2,128)(2,1)S(1)}, u32[]{:S(2)}, u32[]{:S(2)}) async-start(bf16[16,2,4096]{2,1,0:T(2,128)(2,1)} %reshape.64), calls=%async_computation.3 | async-start | bytes 524288 | tf_op jit(solution)/shard_map/all_to_all | solution.py:70
Sparse Core Ops, SparseCore 0:
  127.3 177.2 all-reduce.1
  315.2 25.6 reduce-scatter.2
  345.7 126.7 reduce-scatter.4
